TPU v7x, 128 devices: a whole 4x4x4 slice. The times are simulated.
128 devices in a mesh: clip: 8 (over y_hi, x), tok: 16 (over z, y_lo, core).
Axes of the slice: x: 4, y: 4 (y_hi: 2, y_lo: 2; y = y_hi * 2 + y_lo), z: 4, core: 2. Of those that a mesh axis runs over, the one named last changes fastest.
Arguments:
- features: bfloat16 [2, 20480, 1408], P(None, ('clip', 'tok')), may hold values from -6 to 6
- masked_index: int32 [128, 1408], P(('clip', 'tok')), may hold values from 0 to 1567, as said below
- pos_table: bfloat16 [1568, 512], replicated, may hold values from -6 to 6
- mask_token: bfloat16 [512], replicated, may hold values from -6 to 6
- key_gain: bfloat16 [2, 1408], replicated, may hold values from 0.5 to 1.5
- key_weight: bfloat16 [2, 1408, 1024], replicated, may hold values from -0.15625 to 0.15625
- query_gain: bfloat16 [2, 512], replicated, may hold values from 0.5 to 1.5
- query_weight: bfloat16 [2, 512, 512], replicated, may hold values from -0.25 to 0.25
- out_weight: bfloat16 [2, 512, 512], replicated, may hold values from -0.25 to 0.25
- out_gain: bfloat16 [512], replicated, may hold values from 0.5 to 1.5
- head_weight: bfloat16 [512, 1536], replicated, may hold values from -0.25 to 0.25
- target: bfloat16 [128, 1408, 1536], P(('clip', 'tok')), may hold values from -12 to 12
Outputs:
- loss: float32 [], replicated
- feature_grad: bfloat16 [2, 20480, 1408], P(None, ('clip', 'tok'))
- key_grad: float32 [2, 1408, 1024], P(None, ('clip', 'tok'))
- query_grad: float32 [2, 512, 512], P(None, ('clip', 'tok'))
- out_grad: float32 [2, 512, 512], P(None, ('clip', 'tok'))
- head_grad: float32 [512, 1536], P(('clip', 'tok'))
Inputs may be any that keep to these rules, and one draw needn't show every extreme that they name: `masked_index`: each row lists, increasing, the positions f * 196 + s of one clip's masked tokens: the same 196 - 20 patch positions s in each of the 8 time positions f.
All inputs are finite; a program needn't handle non-finite values.
Results may differ from a plain program's by a relative error of at most 0.013.
Values sent between devices are 32-bit elements; how exact they have to be, the bound alone decides.
A program may use at most 256 MiB of HBM per device.

v0:
```python
import math

import jax
import jax.numpy as jnp
from jax import lax
from jax.sharding import PartitionSpec as P

HEADS = 16
VIS = 160


EPSILON = 1e-06


def normalize(values, scale_gain):
    values = values.astype(jnp.float32)
    center = values - jnp.mean(values, axis=-1, keepdims=True)
    spread = jnp.mean(center * center, axis=-1, keepdims=True)
    return center * lax.rsqrt(spread + EPSILON) * scale_gain.astype(jnp.float32)


def round_twice(values):
    return lax.optimization_barrier(values.astype(jnp.bfloat16)).astype(jnp.float32)


def start_stream(positions, pos_table, mask_token):
    return mask_token.astype(jnp.float32) + pos_table[positions].astype(jnp.float32)


def attend(stream, key_values, scale_gain, query_weight, out_weight, query_probe, out_probe):
    clips, rows, width = stream.shape
    visible = key_values.shape[1]
    head_size = width // HEADS
    normed = normalize(stream, scale_gain).astype(jnp.bfloat16).reshape(clips * rows, width)
    queries = jnp.dot(normed, query_weight, preferred_element_type=jnp.float32) + query_probe
    queries = round_twice(queries).reshape(clips, rows, HEADS, head_size)
    keys = key_values[:, :, :width].reshape(clips, visible, HEADS, head_size)
    values = key_values[:, :, width:].reshape(clips, visible, HEADS, head_size)
    scores = jnp.einsum(
        "crhe,cvhe->chrv", queries, keys, precision=lax.Precision.HIGHEST
    ) / math.sqrt(head_size)
    probs = round_twice(jax.nn.softmax(scores, axis=-1))
    mixed = jnp.einsum("chrv,cvhe->crhe", probs, values, precision=lax.Precision.HIGHEST)
    mixed = mixed.astype(jnp.bfloat16).reshape(clips * rows, width)
    update = jnp.dot(mixed, out_weight, preferred_element_type=jnp.float32) + out_probe
    return (stream + update.reshape(clips, rows, width), (normed, mixed))


def decode(stream, key_values, query_gain, query_weight, out_weight, probes):
    saved = []
    for which_layer in range(len(key_values)):
        stream, kept = attend(
            stream,
            key_values[which_layer],
            query_gain[which_layer],
            query_weight[which_layer],
            out_weight[which_layer],
            probes[2 * which_layer],
            probes[2 * which_layer + 1],
        )
        saved.append(kept)
    return (stream, saved)


def head_energy(stream, out_gain, head_weight, target, head_probe):
    width = stream.shape[-1]
    normed = normalize(stream, out_gain).astype(jnp.bfloat16).reshape(-1, width)
    predicted = jnp.dot(normed, head_weight, preferred_element_type=jnp.float32) + head_probe
    error = predicted - target.astype(jnp.float32).reshape(predicted.shape)
    squared = jnp.sum(error * error)
    return (0.5 * squared, (squared, normed))


def outer_sum(normed, cotangent):
    return lax.dot_general(
        normed,
        cotangent.astype(jnp.bfloat16),
        (((0,), (0,)), ((), ())),
        preferred_element_type=jnp.float32,
    )


def shards(
    features,
    masked_index,
    pos_table,
    mask_token,
    key_gain,
    key_weight,
    query_gain,
    query_weight,
    out_weight,
    out_gain,
    head_weight,
    target,
):
    layers = features.shape[0]
    width = mask_token.shape[0]
    key_values = []
    project_backs = []
    feature_normed = []
    for which_layer in range(layers):

        def project_one(rows, which=which_layer):
            normed_rows = normalize(rows, key_gain[which]).astype(jnp.bfloat16)
            return (
                jnp.dot(normed_rows, key_weight[which], preferred_element_type=jnp.float32),
                normed_rows,
            )

        raw, project_back, normed_rows = jax.vjp(project_one, features[which_layer], has_aux=True)
        key_values.append(round_twice(raw).reshape(-1, VIS, 2 * width))
        project_backs.append(project_back)
        feature_normed.append(normed_rows)
    stream = start_stream(masked_index, pos_table, mask_token)
    clips, rows = (stream.shape[0], stream.shape[1])
    probes = tuple((jnp.zeros((clips * rows, width), jnp.float32) for which in range(2 * layers)))

    def forward(key_values, probes):
        return decode(stream, key_values, query_gain, query_weight, out_weight, probes)

    final, backward, saved = jax.vjp(forward, tuple(key_values), probes, has_aux=True)
    head_probe = jnp.zeros((clips * rows, head_weight.shape[1]), jnp.float32)

    def finish(final_rows, head_probe):
        return head_energy(final_rows, out_gain, head_weight, target, head_probe)

    unused, head_backward, (squared, head_normed) = jax.vjp(finish, final, head_probe, has_aux=True)
    stream_cotangent, head_cotangent = head_backward(jnp.float32(1.0))
    head_part = outer_sum(head_normed, head_cotangent)
    key_grads, probe_grads = backward(stream_cotangent)
    feature_parts = []
    key_list = []
    for which_layer in range(layers):
        rounded = round_twice(key_grads[which_layer].reshape(-1, 2 * width))
        feature_parts.append(project_backs[which_layer](rounded)[0])
        key_list.append(outer_sum(feature_normed[which_layer], rounded))
    feature_grad = jnp.stack(feature_parts)
    query_list = [
        outer_sum(saved[which_layer][0], probe_grads[2 * which_layer])
        for which_layer in range(layers)
    ]
    out_list = [
        outer_sum(saved[which_layer][1], probe_grads[2 * which_layer + 1])
        for which_layer in range(layers)
    ]
    key_grad, query_grad, out_grad, head_wide = (
        lax.psum_scatter(jnp.stack(key_list), ("clip", "tok"), scatter_dimension=1, tiled=True),
        lax.psum_scatter(jnp.stack(query_list), ("clip", "tok"), scatter_dimension=1, tiled=True),
        lax.psum_scatter(jnp.stack(out_list), ("clip", "tok"), scatter_dimension=1, tiled=True),
        lax.psum_scatter(head_part[None], ("clip", "tok"), scatter_dimension=1, tiled=True),
    )
    head_grad = head_wide[0]
    total_squared = lax.psum(squared, ("clip", "tok"))
    count = (
        target.shape[0]
        * target.shape[1]
        * target.shape[2]
        * lax.axis_size("tok")
        * lax.axis_size("clip")
    )
    loss = total_squared / count
    return (loss, feature_grad, key_grad, query_grad, out_grad, head_grad)


def solution(mesh):
    in_specs = (
        P(None, ("clip", "tok"), None),
        P(("clip", "tok"), None),
        P(),
        P(),
        P(),
        P(),
        P(),
        P(),
        P(),
        P(),
        P(),
        P(("clip", "tok"), None, None),
    )
    out_specs = (
        P(),
        P(None, ("clip", "tok"), None),
        P(None, ("clip", "tok"), None),
        P(None, ("clip", "tok"), None),
        P(None, ("clip", "tok"), None),
        P(("clip", "tok"), None),
    )
    return jax.shard_map(shards, mesh=mesh, in_specs=in_specs, out_specs=out_specs, check_vma=False)
```

profile of v0, /device:TPU:0, one launch (start us, length us, event | category | flops | bytes accessed | tf_op | source)
XLA Modules:
  0.0 520.4 jit_solution(16939994941316426618)
XLA Ops:
  8.7 1.3 convert_reduce_fusion
  10.1 1.5 fusion.146
  14.0 2.8 fusion.123
  18.6 2.5 fusion.120
  22.1 5.0 gather_fusion
  29.7 2.2 convolution_convert_fusion.2
  31.9 2.3 copy.42
  34.2 8.4 %fusion.215 = f32[16,1408,160]{1,2,0:T(8,128)} fusion(bf16[1408,16,32]{0,2,1:T(8,128)(2,1)S(1)} %bitcast.302, bf16[160,16,32]{0,2,1:T(8,128)(2,1)} %bitcast.316), kind=kOutput, calls=%fused_computation.259 | convolution fusion | flops 230686720 | bytes 16023552 | tf_op jit(solution)/shard_map/jvp(crhe,cvhe->chrv)/dot_general | solution.py:39
  42.6 18.3 %fusion.211 = (f32[16,1408]{1,0:T(8,128)S(1)}, f32[16,1408,160]{1,2,0:T(8,128)}) fusion(f32[16,1408,160]{1,2,0:T(8,128)} %fusion.215), kind=kOutput, calls=%fused_computation.255 | output fusion | flops 14418079 | bytes 28925952 | tf_op jit(solution)/shard_map/jvp()/sub | solution.py:42
  60.9 9.2 %fusion.32 = bf16[1,16,1408,160]{2,3,1,0:T(8,128)(2,1)} fusion(f32[16,1408,160]{1,2,0:T(8,128)} %get-tuple-element.47, f32[16,1408]{1,0:T(8,128)S(1)} %get-tuple-element.46), kind=kLoop, calls=%fused_computation.45 | loop fusion | flops 7208960 | bytes 21716992 | tf_op jit(solution)/shard_map/jvp()/convert_element_type | solution.py:23
  70.0 4.3 fusion.45
  74.4 1.1 fusion.212
  75.9 1.2 copy-done.2
  79.6 8.1 %fusion.216 = f32[16,1408,160]{1,2,0:T(8,128)} fusion(bf16[1408,16,32]{0,2,1:T(8,128)(2,1)S(1)} %bitcast.304, bf16[160,16,32]{0,2,1:T(8,128)(2,1)} %bitcast.318), kind=kOutput, calls=%fused_computation.260 | convolution fusion | flops 230686720 | bytes 16023552 | tf_op jit(solution)/shard_map/jvp(crhe,cvhe->chrv)/dot_general | solution.py:39
  87.7 18.1 %fusion.213 = (f32[16,1408]{1,0:T(8,128)S(1)}, f32[16,1408,160]{1,2,0:T(8,128)}) fusion(f32[16,1408,160]{1,2,0:T(8,128)} %fusion.216), kind=kOutput, calls=%fused_computation.257 | output fusion | flops 14418079 | bytes 28925952 | tf_op jit(solution)/shard_map/jvp()/sub | solution.py:42
  106.5 9.2 %fusion.33 = bf16[1,16,1408,160]{2,3,1,0:T(8,128)(2,1)} fusion(f32[16,1408,160]{1,2,0:T(8,128)} %get-tuple-element.51, f32[16,1408]{1,0:T(8,128)S(1)} %get-tuple-element.50), kind=kLoop, calls=%fused_computation.46 | loop fusion | flops 7208960 | bytes 21716992 | tf_op jit(solution)/shard_map/jvp()/convert_element_type | solution.py:23
  115.7 4.6 fusion.48
  120.3 1.1 fusion.214
  123.3 4.8 multiply_reduce_fusion.2
  128.1 2.8 multiply_reduce_fusion.4
  130.9 4.4 fusion.40
  136.0 2.0 fusion.119
  139.8 3.3 fusion.22
  143.1 5.0 convert_bitcast_fusion.1
  148.1 9.8 %fusion.7 = f32[16,1408]{1,0:T(8,128)S(1)} fusion(bf16[1,16,1408,160]{2,3,1,0:T(8,128)(2,1)} %convert_bitcast_fusion.1, f32[16,1408,160]{1,2,0:T(8,128)} %get-tuple-element.51, f32[16,1408]{1,0:T(8,128)} %multiply_divide_fusion.1), kind=kLoop, calls=%fused_computation.12 | loop fusion | flops 14395392 | bytes 21807104 | tf_op jit(solution)/shard_map/transpose(jvp())/reduce_sum | solution.py:42
  158.6 15.9 %fusion.202 = f32[16,160,32]{1,2,0:T(8,128)} fusion(bf16[1408,16,32]{0,2,1:T(8,128)(2,1)S(1)} %bitcast.305, bf16[1,16,1408,160]{2,3,1,0:T(8,128)(2,1)} %convert_bitcast_fusion.1, f32[16,1408,160]{1,2,0:T(8,128)} %get-tuple-element.51, f32[16,1408]{1,0:T(8,128)S(1)} %neg.27, f32[16,1408]{1,0:T(8,128)S(1)} %get-tuple-element.50), kind=kOutput, calls=%fused_computation.248 | convolution fusion | flops 1402142720 | bytes 23576576 | tf_op jit(solution)/shard_map/transpose(jvp(crhe,cvhe->chrv))/dot_general | solution.py:39
  174.4 12.5 %convolution_convert_fusion.5 = bf16[16,1408,32]{1,2,0:T(8,128)(2,1)S(1)} fusion(bf16[160,16,32]{0,2,1:T(8,128)(2,1)} %bitcast.319, bf16[1,16,1408,160]{2,3,1,0:T(8,128)(2,1)} %convert_bitcast_fusion.1, f32[16,1408,160]{1,2,0:T(8,128)} %get-tuple-element.51, f32[16,1408]{1,0:T(8,128)} %copy-done.34, f32[16,1408]{1,0:T(8,128)S(1)} %get-tuple-element.50), kind=kOutput, calls=%fused_computation.72 | convolution fusion | flops 1402863616 | bytes 23412736 | tf_op jit(solution)/shard_map/transpose(jvp(crhe,cvhe->chrv))/dot_general | solution.py:39
  187.0 2.0 convolution_bitcast_fusion.2
  192.5 2.0 fusion.113
  195.6 2.4 fusion.26
  198.0 5.0 convert_bitcast_fusion
  203.0 9.6 %fusion.13 = f32[16,1408]{1,0:T(8,128)S(1)} fusion(bf16[1,16,1408,160]{2,3,1,0:T(8,128)(2,1)} %convert_bitcast_fusion, f32[16,1408,160]{1,2,0:T(8,128)} %get-tuple-element.47, f32[16,1408]{1,0:T(8,128)S(1)} %multiply_divide_fusion), kind=kLoop, calls=%fused_computation.18 | loop fusion | flops 14395392 | bytes 21807104 | tf_op jit(solution)/shard_map/transpose(jvp())/reduce_sum | solution.py:42
  212.6 16.1 %fusion.200 = f32[16,160,32]{1,2,0:T(8,128)} fusion(bf16[1408,16,32]{0,2,1:T(8,128)(2,1)S(1)} %bitcast.303, bf16[1,16,1408,160]{2,3,1,0:T(8,128)(2,1)} %convert_bitcast_fusion, f32[16,1408,160]{1,2,0:T(8,128)} %get-tuple-element.47, f32[16,1408]{1,0:T(8,128)S(1)} %neg.29, f32[16,1408]{1,0:T(8,128)S(1)} %get-tuple-element.46), kind=kOutput, calls=%fused_computation.247 | convolution fusion | flops 1402142720 | bytes 23576576 | tf_op jit(solution)/shard_map/transpose(jvp(crhe,cvhe->chrv))/dot_general | solution.py:39
  228.8 12.0 %convolution_convert_fusion.3 = bf16[16,1408,32]{1,2,0:T(8,128)(2,1)S(1)} fusion(bf16[160,16,32]{0,2,1:T(8,128)(2,1)S(1)} %bitcast.317, bf16[1,16,1408,160]{2,3,1,0:T(8,128)(2,1)} %convert_bitcast_fusion, f32[16,1408,160]{1,2,0:T(8,128)} %get-tuple-element.47, f32[16,1408]{1,0:T(8,128)S(1)} %neg.29, f32[16,1408]{1,0:T(8,128)S(1)} %get-tuple-element.46), kind=kOutput, calls=%fused_computation.70 | convolution fusion | flops 1402863616 | bytes 23412736 | tf_op jit(solution)/shard_map/transpose(jvp(crhe,cvhe->chrv))/dot_general | solution.py:39
  242.3 2.0 fusion.116
  244.5 3.6 convolution_bitcast_fusion.1
  248.1 8.8 %pad_maximum_fusion = f32[2,1408,1024]{2,1,0:T(8,128)} fusion(f32[1,1408,1024]{2,1,0:T(8,128)S(1)} %convolution_bitcast_fusion, f32[1,1408,1024]{2,1,0:T(8,128)} %convolution_bitcast_fusion.1), kind=kLoop, calls=%fused_computation.27 | loop fusion | flops 2883584 | bytes 23068672 | tf_op jit(solution)/shard_map/stack | solution.py:148
  256.9 20.5 %copy.47 = f32[2,1408,1024]{2,0,1:T(2,128)} copy(f32[2,1408,1024]{2,1,0:T(8,128)} %pad_maximum_fusion) | data formatting | bytes 23068672 | tf_op jit(solution)/shard_map/stack | solution.py:148
  277.4 1.5 pad_maximum_fusion.2
  279.7 1.5 pad_maximum_fusion.1
  281.2 69.4 %psum.7 = f32[]{:T(128)} all-reduce(f32[]{:T(128)} %get-tuple-element.54), channel_id=1, replica_groups=mesh['clip'=8,'tok'=16] {'clip','tok'}, use_global_device_ids=true, to_apply=%region_15.0 | all-reduce | flops 1 | bytes 8 | tf_op jit(solution)/shard_map/psum | solution.py:154
  351.3 3.0 fusion.93
  354.4 3.2 fusion.135
  359.5 147.0 %all-reduce.11.cloned.1.call-done = (f32[2,1408,1024]{2,0,1:T(2,128)}, f32[2,512,512]{2,1,0:T(8,128)}, f32[2,512,512]{2,1,0:T(8,128)}, f32[1,512,1536]{2,1,0:T(8,128)}) async-done(((f32[2,1408,1024]{2,0,1:T(2,128)}, f32[2,512,512]{2,1,0:T(8,128)}, f32[2,512,512]{2,1,0:T(8,128)}, f32[1,512,1536]{2,1,0:T(8,128)}), (f32[2,1408,1024]{2,0,1:T(2,128)}, f32[2,512,512]{2,1,0:T(8,128)}, f32[2,512,512]{2,1,0:T(8,128)}, ...) | async-done | bytes 18874384
  506.5 1.4 constant_dynamic-slice_fusion.1
  507.9 1.4 constant_dynamic-slice_fusion
  509.2 1.4 dynamic-slice_bitcast_fusion
  510.6 1.5 constant_dynamic-slice_fusion.2
  (188 shorter events, 26.2 us)
Async XLA Ops:
  7.2 15.0 %copy-start = (bf16[1568,512]{1,0:T(8,128)(2,1)S(1)}, bf16[1568,512]{1,0:T(8,128)(2,1)}, u32[]{:S(2)}) copy-start(bf16[1568,512]{1,0:T(8,128)(2,1)} %param.14) | copy-start | bytes 4816900
  7.2 499.3 %all-reduce.11.cloned.1.call-start = ((), (), s32[]{:S(2)}) async-start(), calls=%async_computation | async-start | bytes 37748736
  8.0 66.4 %copy-start.43 = (f32[512]{0:T(512)}, f32[512]{0:T(512)S(1)}, u32[]{:S(2)}) copy-start(f32[512]{0:T(512)S(1)} %convert_element_type.277) | copy-start | bytes 6148
  10.1 6.7 %copy-start.37 = (f32[160]{0:T(256)}, f32[160]{0:T(256)S(1)}, u32[]{:S(2)}) copy-start(f32[160]{0:T(256)S(1)} %get-tuple-element.61) | copy-start | bytes 1924
  10.1 8.5 %copy-start.40 = (f32[160]{0:T(256)}, f32[160]{0:T(256)S(1)}, u32[]{:S(2)}) copy-start(f32[160]{0:T(256)S(1)} %get-tuple-element.62) | copy-start | bytes 1924
  11.6 5.2 copy-start.51
  11.6 5.2 copy-start.53
  11.6 5.2 copy-start.45
  11.7 6.9 %copy-start.48 = (f32[160]{0:T(256)}, f32[160]{0:T(256)S(1)}, u32[]{:S(2)}) copy-start(f32[160]{0:T(256)S(1)} %fusion.193) | copy-start | bytes 1924
  12.4 16.5 %copy-start.57 = (f32[1,512]{1,0:T(1,128)}, f32[1,512]{1,0:T(1,128)S(1)}, u32[]{:S(2)}) copy-start(f32[1,512]{1,0:T(1,128)S(1)} %get-tuple-element.45) | copy-start | bytes 6148
  14.0 2.8 copy-start.32
  14.0 4.6 copy-start.30
  14.0 4.5 copy-start.5
  27.9 46.5 %copy-start.7 = (bf16[1408,512]{0,1:T(8,128)(2,1)}, bf16[1408,512]{0,1:T(8,128)(2,1)S(1)}, u32[]{:S(2)}) copy-start(bf16[1408,512]{0,1:T(8,128)(2,1)S(1)} %copy.40) | copy-start | bytes 4325380
  28.3 3.6 copy-start.35
  28.9 3.0 copy-start.55
  34.2 8.4 %copy-start.9 = (bf16[1408,512]{0,1:T(8,128)(2,1)}, bf16[1408,512]{0,1:T(8,128)(2,1)S(1)}, u32[]{:S(2)}) copy-start(bf16[1408,512]{0,1:T(8,128)(2,1)S(1)} %copy.42) | copy-start | bytes 4325380
  70.0 4.4 copy-start.27
  115.7 4.6 copy-start.3
  115.7 4.6 copy-start.28
  120.3 2.2 slice-start.4
  120.3 2.2 slice-start.5
  135.3 3.7 slice-start.2
  135.9 3.9 slice-start.3
  139.8 3.3 copy-start.13
  174.4 12.6 %copy-start.4 = (f32[1408,512]{0,1:T(8,128)S(1)}, f32[1408,512]{0,1:T(8,128)}, u32[]{:S(2)}) copy-start(f32[1408,512]{0,1:T(8,128)} %copy-done.2) | copy-start | bytes 8650756
  190.2 2.2 copy-start.15
  190.2 5.3 %slice-start = ((s8[7208960]{0:T(1024)(128)(4,1)}), s8[4194304]{0:T(1024)(128)(4,1)S(1)}, s32[]{:S(2)}) async-start(s8[7208960]{0:T(1024)(128)(4,1)} %bitcast.292), calls=%async_computation.1 | async-start | bytes 8388608
  192.5 3.1 slice-start.1
  203.0 9.6 %copy-start.10 = (bf16[1408,512]{0,1:T(8,128)(2,1)S(1)}, bf16[1408,512]{0,1:T(8,128)(2,1)}, u32[]{:S(2)}) copy-start(bf16[1408,512]{0,1:T(8,128)(2,1)} %copy-done.9) | copy-start | bytes 4325380
  212.6 16.1 %copy-start.17 = (bf16[1,160,512]{1,2,0:T(8,128)(2,1)S(1)}, bf16[1,160,512]{1,2,0:T(8,128)(2,1)}, u32[]{:S(2)}) copy-start(bf16[1,160,512]{1,2,0:T(8,128)(2,1)} %copy.43) | copy-start | bytes 491524
  228.8 12.0 %copy-start.16 = (f32[16,32,160]{2,1,0:T(8,128)S(1)}, f32[16,32,160]{2,1,0:T(8,128)}, u32[]{:S(2)}) copy-start(f32[16,32,160]{2,1,0:T(8,128)} %fusion.22) | copy-start | bytes 983044
  228.8 12.1 %copy-start.22 = (f32[16,160,32]{1,2,0:T(8,128)S(1)}, f32[16,160,32]{1,2,0:T(8,128)}, u32[]{:S(2)}) copy-start(f32[16,160,32]{1,2,0:T(8,128)} %fusion.202) | copy-start | bytes 983044
  228.8 12.1 %copy-start.6 = (bf16[2,160,1408]{2,1,0:T(8,128)(2,1)S(1)}, bf16[2,160,1408]{2,1,0:T(8,128)(2,1)}, u32[]{:S(2)}) copy-start(bf16[2,160,1408]{2,1,0:T(8,128)(2,1)} %param.12) | copy-start | bytes 2703364
  228.8 12.1 %copy-start.33 = (f32[1408]{0:T(1024)S(1)}, f32[1408]{0:T(1024)}, u32[]{:S(2)}) copy-start(f32[1408]{0:T(1024)} %copy-done.32) | copy-start | bytes 16900
  228.8 12.1 %copy-start.38 = (f32[160]{0:T(256)S(1)}, f32[160]{0:T(256)}, u32[]{:S(2)}) copy-start(f32[160]{0:T(256)} %copy-done.37) | copy-start | bytes 1924
  228.8 12.1 %copy-start.46 = (f32[160]{0:T(256)S(1)}, f32[160]{0:T(256)}, u32[]{:S(2)}) copy-start(f32[160]{0:T(256)} %copy-done.45) | copy-start | bytes 1924
  242.3 2.1 copy-start.31
  256.9 20.5 %copy-start.18 = (f32[1,512,512]{2,1,0:T(8,128)S(1)}, f32[1,512,512]{2,1,0:T(8,128)}, u32[]{:S(2)}) copy-start(f32[1,512,512]{2,1,0:T(8,128)} %fusion.119) | copy-start | bytes 3145732
  256.9 20.5 %copy-start.20 = (f32[1,512,512]{2,1,0:T(8,128)S(1)}, f32[1,512,512]{2,1,0:T(8,128)}, u32[]{:S(2)}) copy-start(f32[1,512,512]{2,1,0:T(8,128)} %fusion.113) | copy-start | bytes 3145732
  277.4 2.3 copy-start.21
  354.3 3.2 copy-start.54
  354.3 3.2 copy-start.52
  354.3 3.3 copy-start.39
  354.3 3.3 copy-start.42
  354.3 3.3 copy-start.47
  354.3 3.3 copy-start.50
  357.6 154.6 %copy-start.1 = (bf16[1568,512]{1,0:T(8,128)(2,1)S(1)}, bf16[1568,512]{1,0:T(8,128)(2,1)}, u32[]{:S(2)}) copy-start(bf16[1568,512]{1,0:T(8,128)(2,1)} %param.14) | copy-start | bytes 4816900
  (19 other events, 31.0 us)
Sparse Core Ops, SparseCore 0:
  281.3 225.1 all-reduce.10
where the time goes:
time: 527 us; the launch traced here: 520 us
  waiting for transfers between devices  147 us (28%)
  matrix products  143 us (27%)
  other arithmetic  98.2 us (19%)
  blocking collectives  69.4 us (13%)
  local copies, waits for them, and re-layouts  46 us (9%)
  between operations  17.1 us (3%)
    unnamed x2, waiting for transfers between devices  147 us
    dot_general x6, matrix products, attend(): jnp.einsum('crhe,cvhe->chrv', queries, keys, precision=lax.Precision.HIGH...  73 us
    psum x1, blocking collectives, shards(): total_squared = lax.psum(squared, ('clip', 'tok'))  69.4 us
    sub x2, other arithmetic, attend(): probs = round_twice(jax.nn.softmax(scores, axis=-1))  36.3 us
    dot_general x6, matrix products, attend(): jnp.einsum('chrv,cvhe->crhe', probs, values, precision=lax.Precision.HIGH...  24.6 us
    another operation x1, local copies, waits for them, and re-layouts, shards(): jnp.stack(key_list)  20.5 us
    reduce_sum x2, other arithmetic, attend(): probs = round_twice(jax.nn.softmax(scores, axis=-1))  19.4 us
    convert_element_type x4, other arithmetic, round_twice(): values.astype(jnp.bfloat16)  18.5 us
  transfers between devices with their start and end apart: 1, of which 1 were waited for; matrix products, arithmetic and copies ran while one was open for 2% of the time, Pallas kernels for 0%

commit v1 on v0

v1 whole, which is shorter than its diff:
```python
import math

import jax
import jax.numpy as jnp
from jax import lax
from jax.experimental import pallas as pl
from jax.experimental.pallas import tpu as pltpu
from jax.sharding import PartitionSpec as P

HEADS = 16
HS = 32
VIS = 160
D = 1408
DD = 512
PIX = 1536
ROWS = 1408
TOKS = 1568
CH = 256
EXT = 48
EPS = 1e-6
F32 = jnp.float32
BF = jnp.bfloat16
SCALE = 1.0 / math.sqrt(HS)
LOG2 = SCALE * math.log2(math.e)
GF = 4
GB = 2
SLOT = 3072


def nn(a, b):
    return lax.dot_general(a, b, (((1,), (0,)), ((), ())), preferred_element_type=F32)


def nt(a, b):
    return lax.dot_general(a, b, (((1,), (1,)), ((), ())), preferred_element_type=F32)


def wide(g, w):
    return jnp.concatenate([g] * (w // 128), axis=1)


def compute_kernel(
    idx_ref, feat_ref, tok_ref, kgain_ref, qgain_ref, ogain_ref,
    pos_hbm, kw_hbm, qw_hbm, ow_hbm, hw_hbm, tgt_hbm,
    loss_ref, fgrad_ref, g_hbm,
    pos, kw, qw, ow, hw, err, posT, qwT, owT, nf, nfT, k2, vx, vTx, kT, probs0, probs1,
    nq, qs, ms, dus, dqs, no, rs, invs, dx_all, dkvT, gains, q2, dme, stage, esum, sems, gsem,
):
    loads = [
        pltpu.make_async_copy(pos_hbm, pos, sems.at[0]),
        pltpu.make_async_copy(kw_hbm, kw, sems.at[1]),
        pltpu.make_async_copy(qw_hbm, qw, sems.at[2]),
        pltpu.make_async_copy(ow_hbm, ow, sems.at[3]),
        pltpu.make_async_copy(hw_hbm, hw, sems.at[4]),
        pltpu.make_async_copy(tgt_hbm.at[0], err, sems.at[5]),
    ]
    for i in (2, 3, 0, 1, 4, 5):
        loads[i].start()

    for i, row in enumerate((qgain_ref[0:1, :], qgain_ref[1:2, :], ogain_ref[...], tok_ref[...])):
        gains[i] = jnp.broadcast_to(row.astype(F32).reshape(1, DD), (128, DD)).T

    def feature_norm(l):
        f = feat_ref[l].astype(F32)
        c = f - jnp.mean(f, axis=1, keepdims=True)
        r = lax.rsqrt(jnp.mean(c * c, axis=1, keepdims=True) + EPS)
        return c * r, r

    for l in range(2):
        n = (feature_norm(l)[0] * kgain_ref[l:l + 1, :].astype(F32)).astype(BF)
        nf[l] = n
        nfT[l] = n.T
    loads[2].wait()
    loads[3].wait()
    for l in range(2):
        qwT[l] = qw[l].T
        owT[l] = ow[l].T
    loads[0].wait()
    posT[...] = pos[...].T
    loads[1].wait()
    tail = jnp.concatenate([jnp.ones((1, VIS), BF), jnp.zeros((EXT - HS - 1, VIS), BF)], axis=0)
    vtail = jnp.concatenate([jnp.ones((VIS, 2), BF), jnp.zeros((VIS, EXT - HS - 2), BF)], axis=1)
    for l in range(2):
        keys = nn(nf[l], kw[l, :, 0:DD]).astype(BF)
        vals = nn(nf[l], kw[l, :, DD:2 * DD]).astype(BF)
        kT[l] = keys.T
        vT = vals.T
        for h in range(HEADS):
            hs = slice(h * HS, (h + 1) * HS)
            k2[l, h] = jnp.concatenate([keys[:, hs], keys[:, hs]], axis=1)
            vx[l, h] = jnp.concatenate([vals[:, hs], vtail], axis=1)
            vTx[l, h] = jnp.concatenate([vT[hs, :], tail], axis=0)
    dkvT[...] = jnp.zeros_like(dkvT)
    esum[...] = jnp.zeros_like(esum)

    def norm(x, gain):
        c = x - jnp.mean(x, axis=0, keepdims=True)
        r = lax.rsqrt(jnp.mean(c * c, axis=0, keepdims=True) + EPS)
        return (c * r * gain).astype(BF), r

    def norm_back(dy, n, r, gain):
        n = n.astype(F32)
        m2 = jnp.mean(dy * n, axis=0, keepdims=True)
        dxh = dy * gain
        m1 = jnp.mean(dxh, axis=0, keepdims=True)
        return r * (dxh - m1 - n * (m2 / gain))

    def fwd_layer(l, x, t0, w):
        tsl = pl.ds(t0, w)
        n, r = norm(x, wide(gains[l], w))
        nq[l, :, tsl] = n
        rs[l, :, tsl] = r
        qb = nn(qwT[l], n).astype(BF)
        qs[l, :, tsl] = qb
        qf = qb.astype(F32) * LOG2
        hi = qf.astype(BF)
        lo = (qf - hi.astype(F32)).astype(BF)
        q2[:, 0:HS, 0:w] = hi.reshape(HEADS, HS, w)
        q2[:, HS:2 * HS, 0:w] = lo.reshape(HEADS, HS, w)

        def scores(h):
            return nn(k2[l, h], q2[h, :, 0:w])

        def soft(h, s):
            p = jnp.exp2(s - jnp.max(s, axis=0, keepdims=True)).astype(BF)
            if l == 0:
                probs0[h, :, tsl] = p
            else:
                probs1[h, :, 0:w] = p
            return p

        def mix(h, p):
            o = nn(vTx[l, h], p)
            inv = 1.0 / o[HS:HS + 1]
            invs[l, h:h + 1, tsl] = inv
            ms[l, h * HS:(h + 1) * HS, tsl] = (o[:HS] * inv).astype(BF)

        n_g = HEADS // GF
        s = [scores(u) for u in range(GF)]
        before = None
        for g in range(n_g):
            s2 = [scores((g + 1) * GF + u) for u in range(GF)] if g + 1 < n_g else None
            ps = [soft(g * GF + u, s[u]) for u in range(GF)]
            if before is not None:
                for u in range(GF):
                    mix((g - 1) * GF + u, before[u])
            s, before = s2, ps
        for u in range(GF):
            mix((n_g - 1) * GF + u, before[u])
        return x + nn(owT[l], ms[l, :, tsl])

    def bwd_layer(l, dx, t0, w):
        tsl = pl.ds(t0, w)
        du = dx.astype(BF)
        dus[:, tsl] = du
        dm = nn(ow[l], du).reshape(HEADS, HS, w) * invs[l, :, tsl].reshape(HEADS, 1, w)
        dm = dm.astype(BF)
        dme[:, 0:HS, 0:w] = dm
        dsum = jnp.sum(dm.astype(F32) * ms[l, :, tsl].astype(F32).reshape(HEADS, HS, w), axis=1, keepdims=True)
        hi = dsum.astype(BF)
        lo = (dsum - hi.astype(F32)).astype(BF)
        dme[:, HS:EXT, 0:w] = jnp.concatenate([-hi, -lo, jnp.zeros((HEADS, EXT - HS - 2, w), BF)], axis=1)

        def probs(h):
            return probs0[h, :, tsl] if l == 0 else probs1[h, :, 0:w]

        def dprobs(h):
            return nn(vx[l, h], dme[h, :, 0:w])

        def dscores(h, x):
            return (probs(h).astype(F32) * x).astype(BF)

        def rest(h, ds):
            hs = slice(h * HS, (h + 1) * HS)
            vs = slice(DD + h * HS, DD + (h + 1) * HS)
            dqs[hs, tsl] = (nn(kT[l, hs, :], ds) * SCALE).astype(BF)
            dkvT[l, hs, :] += nt(qs[l, hs, tsl], ds)
            dkvT[l, vs, :] += nt(dme[h, 0:HS, 0:w], probs(h))

        n_g = HEADS // GB
        x = [dprobs(u) for u in range(GB)]
        before = None
        for g in range(n_g):
            x2 = [dprobs((g + 1) * GB + u) for u in range(GB)] if g + 1 < n_g else None
            ds = [dscores(g * GB + u, x[u]) for u in range(GB)]
            if before is not None:
                for u in range(GB):
                    rest((g - 1) * GB + u, before[u])
            x, before = x2, ds
        for u in range(GB):
            rest((n_g - 1) * GB + u, before[u])

        dn = nn(qw[l], dqs[:, tsl])
        return dx + norm_back(dn, nq[l, :, tsl], rs[l, :, tsl], wide(gains[l], w))

    def chunk_a(t0, w):
        tsl = pl.ds(t0, w)
        ids = idx_ref[:, tsl]
        onehot = (lax.broadcasted_iota(jnp.int32, (TOKS, w), 0) == ids).astype(BF)
        x = wide(gains[3], w) + nn(posT[...], onehot)
        x = fwd_layer(0, x, t0, w)
        x = fwd_layer(1, x, t0, w)
        n, r = norm(x, wide(gains[2], w))
        no[:, tsl] = n
        nT = n.T
        e = nn(nT, hw[...]) - err[tsl, :].astype(F32)
        esum[...] += jnp.sum(e * e, axis=0, keepdims=True)
        eb = e.astype(BF)
        err[tsl, :] = eb
        dn = nt(hw[...], eb)
        dx = norm_back(dn, n, r, wide(gains[2], w))
        dx_all[:, tsl] = bwd_layer(1, dx, t0, w)

    def chunk_b(t0, w):
        tsl = pl.ds(t0, w)
        bwd_layer(0, dx_all[:, tsl], t0, w)

    loads[4].wait()
    loads[5].wait()
    full = ROWS // CH
    rem = ROWS - full * CH

    @pl.loop(0, full)
    def _(i):
        chunk_a(pl.multiple_of(i * CH, CH), CH)

    chunk_a(full * CH, rem)

    loss_ref[...] = jnp.full((8, 128), jnp.sum(esum[...]), F32)

    pending = [[], []]
    count = [0]

    def emit(dot, lhs, rhs, rows, width, share, dsts):
        slot = count[0] % 2
        count[0] += 1
        for cp in pending[slot]:
            cp.wait()
        parts = width // 128
        for c in range(width // 256):
            block = dot(lhs, rhs(c * 256))
            for j in range(2):
                stage[slot, pl.ds(2 * c + j, rows, stride=parts), :] = block[:, j * 128:(j + 1) * 128]
        n = rows * parts
        src = stage.at[slot, pl.ds(0, n)].reshape(n // share, share, 128)
        pending[slot] = []
        for i, (lo, hi, dst) in enumerate(dsts):
            cp = pltpu.make_async_copy(src.at[:, pl.ds(lo, hi - lo)], dst, gsem.at[slot, i])
            cp.start()
            pending[slot].append(cp)

    def grads_layer(l):
        emit(nt, nq[l], lambda c: dqs[c:c + 256, :], DD, DD, 16, [(0, 16, g_hbm.at[2, :, pl.ds(16 * l, 16)])])
        emit(nt, ms[l], lambda c: dus[c:c + 256, :], DD, DD, 16, [(0, 16, g_hbm.at[2, :, pl.ds(32 + 16 * l, 16)])])
        dkvT[l, 0:DD, :] = dkvT[l, 0:DD, :] * SCALE
        dT = dkvT[l].astype(BF)
        for b in range(4):
            emit(nt, nfT[l, b * 352:(b + 1) * 352, :], lambda c: dT[c:c + 256, :], 352, 2 * DD, 88,
                 [(0, 88, g_hbm.at[l, pl.ds(32 * b, 32), pl.ds(0, 88)])])
        d = dkvT[l].T.astype(BF)
        dn = nt(d, kw[l])
        xh, r = feature_norm(l)
        dxh = dn * kgain_ref[l:l + 1, :].astype(F32)
        m1 = jnp.mean(dxh, axis=1, keepdims=True)
        m2 = jnp.mean(dxh * xh, axis=1, keepdims=True)
        fgrad_ref[l] = (r * (dxh - m1 - xh * m2)).astype(BF)

    for b in range(2):
        to = pl.ds(64 * b, 64)
        emit(nn, no[b * 256:(b + 1) * 256, :], lambda c: err[:, c:c + 256], 256, PIX, 48, [
            (0, 8, g_hbm.at[0, to, pl.ds(88, 8)]),
            (8, 16, g_hbm.at[1, to, pl.ds(88, 8)]),
            (16, 48, g_hbm.at[2, to, pl.ds(64, 32)])])
    grads_layer(1)

    @pl.loop(0, full)
    def _(i):
        chunk_b(pl.multiple_of(i * CH, CH), CH)

    chunk_b(full * CH, rem)
    grads_layer(0)
    for cp in pending[0] + pending[1]:
        cp.wait()


def compute(features, masked_index, pos_table, mask_token, key_gain, key_weight, query_gain,
            query_weight, out_weight, out_gain, head_weight, target):
    vm = pl.BlockSpec(memory_space=pltpu.VMEM)
    hb = pl.BlockSpec(memory_space=pl.ANY)
    out_shape = (
        jax.ShapeDtypeStruct((8, 128), F32),
        jax.ShapeDtypeStruct((2, VIS, D), BF),
        jax.ShapeDtypeStruct((3, 128, 96, 128), F32),
    )
    V = pltpu.VMEM
    scratch = [
        V((TOKS, DD), BF), V((2, D, 2 * DD), BF), V((2, DD, DD), BF), V((2, DD, DD), BF), V((DD, PIX), BF),
        V((ROWS, PIX), BF), V((DD, TOKS), BF), V((2, DD, DD), BF), V((2, DD, DD), BF),
        V((2, VIS, D), BF), V((2, D, VIS), BF),
        V((2, HEADS, VIS, 2 * HS), BF), V((2, HEADS, VIS, EXT), BF), V((2, HEADS, EXT, VIS), BF), V((2, DD, VIS), BF),
        V((HEADS, VIS, ROWS), BF), V((HEADS, VIS, CH), BF),
        V((2, DD, ROWS), BF), V((2, DD, ROWS), BF), V((2, DD, ROWS), BF), V((DD, ROWS), BF), V((DD, ROWS), BF),
        V((DD, ROWS), BF), V((2, 1, ROWS), F32), V((2, HEADS, ROWS), F32), V((DD, ROWS), F32), V((2, 2 * DD, VIS), F32),
        V((4, DD, 128), F32), V((HEADS, 2 * HS, CH), BF), V((HEADS, EXT, CH), BF),
        V((2, SLOT, 128), F32), V((1, PIX), F32),
        pltpu.SemaphoreType.DMA((6,)), pltpu.SemaphoreType.DMA((2, 3)),
    ]
    return pl.pallas_call(
        compute_kernel,
        out_shape=out_shape,
        in_specs=[vm] * 6 + [hb] * 6,
        out_specs=[vm, vm, hb],
        scratch_shapes=scratch,
        compiler_params=pltpu.CompilerParams(vmem_limit_bytes=63 * 1024 * 1024),
        name="decode",
    )(
        masked_index, features, mask_token.reshape(1, DD), key_gain, query_gain, out_gain.reshape(1, DD),
        pos_table, key_weight, query_weight, out_weight, head_weight, target,
    )


MESH = pl.DeviceIdType.MESH
PARTS = 3
PROWS = 96
ORDERS = (("x", "y", "z"), ("y", "z", "x"), ("z", "x", "y"))


def part_index(coords):
    y = coords["y"]
    if isinstance(y, slice):
        return (y, coords["x"], coords["z"], y)
    return (y // 2, coords["x"], coords["z"], y % 2)


def block_shape(free):
    shape = []
    for name, size in (("y", 2), ("x", 4), ("z", 4), ("y", 2)):
        if name in free:
            shape.append(size)
    return tuple(shape)


def reduce_kernel(g_ref, loss_ref, k_out, q_out, o_out, h_out, l_out, own, got, lbuf, *rest):
    n_stage = 9
    first = rest[0:n_stage]
    second = rest[n_stage:2 * n_stage]
    send, recv, lsem = rest[2 * n_stage:]
    clip, tok = lax.axis_index("clip"), lax.axis_index("tok")
    me = {"x": clip % 4, "y": (clip // 4) * 2 + (tok // 2) % 2, "z": tok // 4}
    core = tok % 2

    def device(c, k):
        return ((c["y"] // 2) * 4 + c["x"], c["z"] * 4 + (c["y"] % 2) * 2 + k)

    def shifted(axis, by):
        c = dict(me)
        c[axis] = (me[axis] + by + 4) % 4
        return c

    partner = device(me, 1 - core)
    sides = {a: (device(shifted(a, 1), core), device(shifted(a, -1), core)) for a in "xyz"}

    barrier = pltpu.get_barrier_semaphore()
    for dev in [partner] + [d for a in "xyz" for d in sides[a]]:
        pl.semaphore_signal(barrier, inc=1, device_id=dev, device_id_type=MESH)
    pl.semaphore_wait(barrier, 7)

    counter = [0]

    def remote(src, dst, dev):
        i = counter[0]
        counter[0] += 1
        cp = pltpu.make_async_remote_copy(
            src_ref=src, dst_ref=dst, send_sem=send.at[i], recv_sem=recv.at[i], device_id=dev, device_id_type=MESH)
        cp.start()
        return cp

    full = slice(None)

    def coords_of(part, stage, j):
        c = {}
        for s, a in enumerate(ORDERS[part]):
            c[a] = me[a] if s < stage else (j if s == stage else full)
        return c

    def each(part, stage, body):
        free = [a for s, a in enumerate(ORDERS[part]) if s > stage]

        @pl.loop(0, 4 ** len(free))
        def _(i):
            c = {}
            for a in free:
                c[a] = i % 4
                i = i // 4
            body(c)

    def pick(part, stage, j, c):
        at = coords_of(part, stage, j)
        at.update(c)
        return (part,) + part_index(at)

    def place(part, stage, c):
        free = [a for s, a in enumerate(ORDERS[part]) if s > stage]
        out = []
        for name in ("yh", "x", "z", "yl"):
            if name[0] in free:
                out.append(c["y"] // 2 if name == "yh" else c["y"] % 2 if name == "yl" else c[name])
        return tuple(out)

    mine, swaps = {}, {}
    k = 0
    for by in (2, 1, 3, 0):
        for part in range(PARTS):
            a = ORDERS[part][0]
            at = coords_of(part, 0, (me[a] + by) % 4)
            yh, x, z, yl = part_index(at)
            swaps[part, by] = remote(g_ref.at[part, yh, x, z, yl, 1 - core], got.at[part, yh, x, z, yl], partner)
            cp = pltpu.make_async_copy(g_ref.at[part, yh, x, z, yl, core], own.at[part, yh, x, z, yl], lsem.at[k])
            cp.start()
            mine[part, by] = cp
            k += 1

    def add_swap(part, by):
        a = ORDERS[part][0]
        j = (me[a] + by) % 4
        mine[part, by].wait()
        swaps[part, by].wait_recv()

        def body(c):
            i = pick(part, 0, j, c)
            own[i] = own[i] + got[i]
        each(part, 0, body)

    lbuf[0, core] = loss_ref[...]
    lcopy = remote(loss_ref, lbuf.at[0, core], partner)

    for stage in range(3):
        axis = ["x", "y", "z"][stage]
        if stage == 0:
            for part in range(PARTS):
                add_swap(part, 2)
        steps = []
        for part in range(PARTS):
            a = ORDERS[part][stage]
            buf = first[stage * 3 + part]
            src = own.at[(part,) + part_index(coords_of(part, stage, (me[a] + 2) % 4))]
            pre = (full,) * len(block_shape([b for s, b in enumerate(ORDERS[part]) if s > stage]))
            steps.append((
                remote(src.at[pre + (pl.ds(0, 48),)], buf.at[0], sides[a][0]),
                remote(src.at[pre + (pl.ds(48, 48),)], buf.at[1], sides[a][1])))
        if stage == 0:
            lcopy.wait()
            tile = lbuf[0, 0] + lbuf[0, 1]
        else:
            tile = lbuf[stage, 0] + lbuf[stage, 1] + lbuf[stage, 2] + lbuf[stage, 3]
        lbuf[stage + 1, me[axis]] = tile
        mine_l = lbuf.at[stage + 1, me[axis]]
        l_steps = [remote(mine_l, mine_l, sides[axis][0]), remote(mine_l, mine_l, sides[axis][1])]
        if stage == 0:
            for by in (1, 3):
                for part in range(PARTS):
                    add_swap(part, by)
        steps2 = []
        for part in range(PARTS):
            a = ORDERS[part][stage]
            steps[part][0].wait_recv()
            steps[part][1].wait_recv()
            buf = first[stage * 3 + part]

            def body(c):
                r = pick(part, stage, (me[a] + 1) % 4, c)
                l = pick(part, stage, (me[a] + 3) % 4, c)
                p = place(part, stage, c)
                own[r + (pl.ds(0, 48),)] = own[r + (pl.ds(0, 48),)] + buf[(0,) + p]
                own[l + (pl.ds(48, 48),)] = own[l + (pl.ds(48, 48),)] + buf[(1,) + p]
            each(part, stage, body)
            out = second[stage * 3 + part]
            steps2.append((
                remote(own.at[(part,) + part_index(coords_of(part, stage, (me[a] + 1) % 4))], out.at[0], sides[a][0]),
                remote(own.at[(part,) + part_index(coords_of(part, stage, (me[a] + 3) % 4))], out.at[1], sides[a][1])))
        l_steps[0].wait()
        l_steps[1].wait()
        left = (me[axis] + 3) % 4
        far = lbuf.at[stage + 1, left]
        l_far = remote(far, far, sides[axis][0])
        if stage == 0:
            for part in range(PARTS):
                add_swap(part, 0)
        for part in range(PARTS):
            a = ORDERS[part][stage]
            steps2[part][0].wait_recv()
            steps2[part][1].wait_recv()
            out = second[stage * 3 + part]

            def body(c):
                i = pick(part, stage, me[a], c)
                p = place(part, stage, c)
                own[i] = own[i] + out[(0,) + p] + out[(1,) + p]
            each(part, stage, body)
        l_far.wait()
        for pair in steps + steps2:
            pair[0].wait_send()
            pair[1].wait_send()
    for cp in swaps.values():
        cp.wait_send()

    l_out[...] = lbuf[3, 0] + lbuf[3, 1] + lbuf[3, 2] + lbuf[3, 3]
    at = part_index(me)
    for l in range(2):
        for j in range(8):
            k_out[l, :, j * 128:(j + 1) * 128] = own[(l,) + at + (pl.ds(j, 11, stride=8),)]
        for j in range(4):
            q_out[l, :, j * 128:(j + 1) * 128] = own[(2,) + at + (pl.ds(16 * l + j, 4, stride=4),)]
            o_out[l, :, j * 128:(j + 1) * 128] = own[(2,) + at + (pl.ds(32 + 16 * l + j, 4, stride=4),)]
    for r in range(4):
        for j in range(12):
            i = r * 12 + j
            part, row = (0, 88 + i) if i < 8 else (1, 80 + i) if i < 16 else (2, 48 + i)
            h_out[r:r + 1, j * 128:(j + 1) * 128] = own[(part,) + at + (pl.ds(row, 1),)]


def reduce_scatter(g, loss):
    V = pltpu.VMEM
    vm = pl.BlockSpec(memory_space=pltpu.VMEM)
    scratch = [V((PARTS, 2, 4, 4, 2, PROWS, 128), F32), V((PARTS, 2, 4, 4, 2, PROWS, 128), F32), V((4, 4, 8, 128), F32)]
    for rows in (48, PROWS):
        for stage in range(3):
            for part in range(PARTS):
                shape = block_shape(ORDERS[part][stage + 1:])
                scratch.append(V((2,) + shape + (rows, 128), F32))
    n_copies = 12 + 1 + 3 * (12 + 3)
    scratch += [pltpu.SemaphoreType.DMA((n_copies,)), pltpu.SemaphoreType.DMA((n_copies,)), pltpu.SemaphoreType.DMA((12,))]
    return pl.pallas_call(
        reduce_kernel,
        out_shape=(
            jax.ShapeDtypeStruct((2, 11, 2 * DD), F32),
            jax.ShapeDtypeStruct((2, 4, DD), F32),
            jax.ShapeDtypeStruct((2, 4, DD), F32),
            jax.ShapeDtypeStruct((4, PIX), F32),
            jax.ShapeDtypeStruct((8, 128), F32),
        ),
        in_specs=[pl.BlockSpec(memory_space=pl.ANY), vm],
        out_specs=[vm] * 5,
        scratch_shapes=scratch,
        compiler_params=pltpu.CompilerParams(
            collective_id=0, has_side_effects=True, vmem_limit_bytes=60 * 1024 * 1024),
        name="reduce",
    )(g.reshape(PARTS, 2, 4, 4, 2, 2, PROWS, 128), loss)


def shards(features, masked_index, pos_table, mask_token, key_gain, key_weight, query_gain,
           query_weight, out_weight, out_gain, head_weight, target):
    loss, feature_grad, g = compute(
        features, masked_index, pos_table, mask_token, key_gain, key_weight, query_gain,
        query_weight, out_weight, out_gain, head_weight, target)
    key_grad, query_grad, out_grad, head_grad, total = reduce_scatter(g, loss)
    devices = lax.axis_size("tok") * lax.axis_size("clip")
    return total[0, 0] / (devices * ROWS * PIX), feature_grad, key_grad, query_grad, out_grad, head_grad


def solution(mesh):
    both = ("clip", "tok")
    in_specs = (
        P(None, both, None), P(both, None), P(), P(), P(), P(), P(), P(), P(), P(), P(), P(both, None, None))
    out_specs = (
        P(), P(None, both, None), P(None, both, None), P(None, both, None), P(None, both, None), P(both, None))
    return jax.shard_map(shards, mesh=mesh, in_specs=in_specs, out_specs=out_specs, check_vma=False)
```

time: 527 us -> 158 us (0.30); the launches traced: 520 us -> 157 us
  waiting for transfers between devices: 147 us -> 0 us
  Pallas kernels: 0 us -> 146 us
  matrix products: 143 us -> 0 us
  other arithmetic: 98.2 us -> 0 us
  blocking collectives: 69.4 us -> 0 us
  local copies, waits for them, and re-layouts: 46 us -> 9.32 us
  between operations: 17.1 us -> 2.43 us
    unnamed x2 -> x0, waiting for transfers between devices: 147 us -> none
    pallas_call x0 -> x2, Pallas kernels: none -> 146 us  [the longest x1 81.7 us: compute(): pl.pallas_call(compute_kernel, out_shape=out_shape, in_specs=[vm] * 6 + [...]
    dot_general x32 -> x0, matrix products: 143 us -> none  [the longest x6 73 us: attend(): jnp.einsum('crhe,cvhe->chrv', queries, keys, precision=lax.Precision.HIGH...]
    psum x1 -> x0, blocking collectives: 69.4 us -> none  [shards(): total_squared = lax.psum(squared, ('clip', 'tok'))]
    sub x2 -> x0, other arithmetic: 36.3 us -> none  [attend(): probs = round_twice(jax.nn.softmax(scores, axis=-1))]
    reduce_sum x11 -> x0, other arithmetic: 25.7 us -> none  [the longest x2 19.4 us: attend(): probs = round_twice(jax.nn.softmax(scores, axis=-1))]
    convert_element_type x7 -> x0, other arithmetic: 20.8 us -> none  [the longest x4 18.5 us: round_twice(): values.astype(jnp.bfloat16)]
    another operation x1 -> x0, local copies, waits for them, and re-layouts: 20.5 us -> none  [shards(): jnp.stack(key_list)]
  transfers between devices with their start and end apart: 1 -> 0, of which waited for: 1 -> 0; matrix products, arithmetic and copies ran while one was open for 2% -> 0% of each run, Pallas kernels for 0% -> 0%
where the time goes in v1:
time: 158 us; the launch traced here: 157 us
  Pallas kernels  146 us (92%)
  local copies, waits for them, and re-layouts  9.32 us (6%)
  between operations  2.43 us (2%)
    pallas_call x1, Pallas kernels, compute(): pl.pallas_call(compute_kernel, out_shape=out_shape, in_specs=[vm] * 6 + [...  81.7 us
    pallas_call x1, Pallas kernels, reduce_scatter(): pl.pallas_call(reduce_kernel, out_shape=(jax.ShapeDtypeStruct((2, 11, 2 *...  63.8 us
    unnamed x4, local copies, waits for them, and re-layouts  5.6 us

profile of v1, /device:TPU:0, one launch (start us, length us, event | category | flops | bytes accessed | tf_op | source)
XLA Modules:
  0.0 157.3 jit_solution(5286618461648539969)
XLA Ops:
  0.6 1.3 reshape.23.tok_ref
  1.9 1.3 reshape.24.ogain_ref
  3.2 81.7 %decode.1 = (f32[8,128]{1,0:T(8,128)}, bf16[2,160,1408]{2,1,0:T(8,128)(2,1)}, f32[3,128,96,128]{3,2,1,0:T(8,128)}) custom-call(s32[1,1408]{1,0:T(1,128)} %idx_ref.1, bf16[2,160,1408]{2,1,0:T(8,128)(2,1)} %feat_ref.1, bf16[1,512]{1,0:T(2,128)(2,1)} %reshape.23.tok_ref, bf16[2,1408]{1,0:T(2,128)(2,1)} %kgain_ref.1, bf16[2,512]{1,0:T(2,128)(2,1)} %qgain_ref.1, ...), custom_call_target="tpu_custom_call" | custom-call | tf_op jit(solution)/shard_map/decode/pallas_call | solution.py:308
  84.9 63.8 %reduce.1 = (f32[2,11,1024]{2,1,0:T(8,128)}, f32[2,4,512]{2,1,0:T(4,128)}, f32[2,4,512]{2,1,0:T(4,128)}, f32[4,1536]{1,0:T(4,128)}, f32[8,128]{1,0:T(8,128)}) custom-call(f32[3,2,4,4,2,2,96,128]{7,6,5,4,3,2,1,0:T(8,128)} %bitcast.2, f32[8,128]{1,0:T(8,128)} %get-tuple-element.15.loss_ref), custom_call_target="tpu_custom_call" | custom-call | tf_op jit(solution)/shard_map/reduce/pallas_call | solution.py:533
  148.8 1.2 slice.3
  150.6 1.6 %copy.18 = f32[2,11,1024]{2,0,1:T(2,128)} copy(f32[2,11,1024]{2,1,0:T(8,128)} %get-tuple-element.24) | data formatting | bytes 180224
  152.2 1.3 copy.22
  153.5 1.3 copy.23
  154.9 1.3 copy.24

commit v2 on v1

v2 whole, which is shorter than its diff:
```python
import math

import jax
import jax.numpy as jnp
from jax import lax
from jax.experimental import pallas as pl
from jax.experimental.pallas import tpu as pltpu
from jax.sharding import PartitionSpec as P

HEADS = 16
HS = 32
VIS = 160
D = 1408
DD = 512
PIX = 1536
ROWS = 1408
TOKS = 1568
CH = 256
EXT = 48
EPS = 1e-6
F32 = jnp.float32
BF = jnp.bfloat16
SCALE = 1.0 / math.sqrt(HS)
LOG2 = SCALE * math.log2(math.e)
GF = 4
GB = 2
SLOT = 3072
NCH = 6


def nn(a, b):
    return lax.dot_general(a, b, (((1,), (0,)), ((), ())), preferred_element_type=F32)


def nt(a, b):
    return lax.dot_general(a, b, (((1,), (1,)), ((), ())), preferred_element_type=F32)


def wide(g, w):
    return jnp.concatenate([g] * (w // 128), axis=1)


def norm(x, gain):
    c = x - jnp.mean(x, axis=0, keepdims=True)
    r = lax.rsqrt(jnp.mean(c * c, axis=0, keepdims=True) + EPS)
    return (c * r * gain).astype(BF), r


def norm_back(dy, n, r, gain):
    n = n.astype(F32)
    m2 = jnp.mean(dy * n, axis=0, keepdims=True)
    dxh = dy * gain
    m1 = jnp.mean(dxh, axis=0, keepdims=True)
    return r * (dxh - m1 - n * (m2 / gain))


def feature_norm(feat_ref, l):
    f = feat_ref[l].astype(F32)
    c = f - jnp.mean(f, axis=1, keepdims=True)
    r = lax.rsqrt(jnp.mean(c * c, axis=1, keepdims=True) + EPS)
    return c * r, r


def attention_back(du, w, tsl, ow, invs, ms, probs, vx, kT, qs, dme, dqs, dkvT):
    dm = nn(ow[...], du).reshape(HEADS, HS, w) * invs[:, tsl].reshape(HEADS, 1, w)
    dm = dm.astype(BF)
    dme[:, 0:HS, 0:w] = dm
    dsum = jnp.sum(dm.astype(F32) * ms[:, tsl].astype(F32).reshape(HEADS, HS, w), axis=1, keepdims=True)
    hi = dsum.astype(BF)
    lo = (dsum - hi.astype(F32)).astype(BF)
    dme[:, HS:EXT, 0:w] = jnp.concatenate([-hi, -lo, jnp.zeros((HEADS, EXT - HS - 2, w), BF)], axis=1)

    def dprobs(h):
        return nn(vx[h], dme[h, :, 0:w])

    def dscores(h, x):
        return (probs(h).astype(F32) * x).astype(BF)

    def rest(h, ds):
        hs = slice(h * HS, (h + 1) * HS)
        vs = slice(DD + h * HS, DD + (h + 1) * HS)
        dqs[hs, tsl] = (nn(kT[hs, :], ds) * SCALE).astype(BF)
        dkvT[hs, :] += nt(qs[hs, tsl], ds)
        dkvT[vs, :] += nt(dme[h, 0:HS, 0:w], probs(h))

    n_g = HEADS // GB
    x = [dprobs(u) for u in range(GB)]
    before = None
    for g in range(n_g):
        x2 = [dprobs((g + 1) * GB + u) for u in range(GB)] if g + 1 < n_g else None
        ds = [dscores(g * GB + u, x[u]) for u in range(GB)]
        if before is not None:
            for u in range(GB):
                rest((g - 1) * GB + u, before[u])
        x, before = x2, ds
    for u in range(GB):
        rest((n_g - 1) * GB + u, before[u])


def make_emit(stage, gsem):
    pending = [[], []]
    count = [0]

    def emit(dot, lhs, rhs, rows, width, share, dsts):
        slot = count[0] % 2
        count[0] += 1
        for cp in pending[slot]:
            cp.wait()
        parts = width // 128
        for c in range(width // 256):
            block = dot(lhs, rhs(c * 256))
            for j in range(2):
                stage[slot, pl.ds(2 * c + j, rows, stride=parts), :] = block[:, j * 128:(j + 1) * 128]
        n = rows * parts
        src = stage.at[slot, pl.ds(0, n)].reshape(n // share, share, 128)
        pending[slot] = []
        for i, (lo, hi, dst) in enumerate(dsts):
            cp = pltpu.make_async_copy(src.at[:, pl.ds(lo, hi - lo)], dst, gsem.at[slot, i])
            cp.start()
            pending[slot].append(cp)

    def finish():
        for cp in pending[0] + pending[1]:
            cp.wait()
        pending[0], pending[1] = [], []

    return emit, finish


def compute_kernel(
    idx_ref, feat_ref, tok_ref, kgain_ref, qgain_ref, ogain_ref,
    pos_hbm, kw_hbm, qw_hbm, ow_hbm, hw_hbm, tgt_hbm,
    loss_ref, g0_hbm, g1_hbm, g2_hbm, nq_hbm, qs_hbm, ms_hbm, dus_hbm, probs_hbm, invs_hbm,
    kT_hbm, vx_hbm, nfT_hbm, d_hbm,
    pos, kw, qw, ow, hw, err, posT, qwT, owT, nf, nfT, k2, vx, vTx, kT, probs0, probs1,
    nq, qs, ms, dus, dqs, no, rs, invs, dkvT, gains, q2, dme, stage, esum, dT, sems, gsem, csem, ksem,
):
    loads = [
        pltpu.make_async_copy(pos_hbm, pos, sems.at[0]),
        pltpu.make_async_copy(kw_hbm, kw, sems.at[1]),
        pltpu.make_async_copy(qw_hbm, qw, sems.at[2]),
        pltpu.make_async_copy(ow_hbm, ow, sems.at[3]),
        pltpu.make_async_copy(hw_hbm, hw, sems.at[4]),
        pltpu.make_async_copy(tgt_hbm.at[0], err, sems.at[5]),
    ]
    for i in (2, 3, 0, 1, 4, 5):
        loads[i].start()

    for i, row in enumerate((qgain_ref[0:1, :], qgain_ref[1:2, :], ogain_ref[...], tok_ref[...])):
        gains[i] = jnp.broadcast_to(row.astype(F32).reshape(1, DD), (128, DD)).T

    for l in range(2):
        n = (feature_norm(feat_ref, l)[0] * kgain_ref[l:l + 1, :].astype(F32)).astype(BF)
        nf[l] = n
        nfT[l] = n.T
    loads[2].wait()
    loads[3].wait()
    for l in range(2):
        qwT[l] = qw[l].T
        owT[l] = ow[l].T
    loads[0].wait()
    posT[...] = pos[...].T
    loads[1].wait()
    tail = jnp.concatenate([jnp.ones((1, VIS), BF), jnp.zeros((EXT - HS - 1, VIS), BF)], axis=0)
    vtail = jnp.concatenate([jnp.ones((VIS, 2), BF), jnp.zeros((VIS, EXT - HS - 2), BF)], axis=1)
    for l in range(2):
        keys = nn(nf[l], kw[l, :, 0:DD]).astype(BF)
        vals = nn(nf[l], kw[l, :, DD:2 * DD]).astype(BF)
        kT[l] = keys.T
        vT = vals.T
        for h in range(HEADS):
            hs = slice(h * HS, (h + 1) * HS)
            k2[l, h] = jnp.concatenate([keys[:, hs], keys[:, hs]], axis=1)
            vx[l, h] = jnp.concatenate([vals[:, hs], vtail], axis=1)
            vTx[l, h] = jnp.concatenate([vT[hs, :], tail], axis=0)
    keep = [
        pltpu.make_async_copy(kT.at[0], kT_hbm, ksem.at[0]),
        pltpu.make_async_copy(vx.at[0], vx_hbm, ksem.at[1]),
        pltpu.make_async_copy(nfT.at[0], nfT_hbm, ksem.at[2]),
    ]
    for cp in keep:
        cp.start()
    dkvT[...] = jnp.zeros_like(dkvT)
    esum[...] = jnp.zeros_like(esum)

    def fwd_layer(l, x, t0, w):
        tsl = pl.ds(t0, w)
        n, r = norm(x, wide(gains[l], w))
        nq[l, :, tsl] = n
        rs[l, :, tsl] = r
        qb = nn(qwT[l], n).astype(BF)
        qs[l, :, tsl] = qb
        qf = qb.astype(F32) * LOG2
        hi = qf.astype(BF)
        lo = (qf - hi.astype(F32)).astype(BF)
        q2[:, 0:HS, 0:w] = hi.reshape(HEADS, HS, w)
        q2[:, HS:2 * HS, 0:w] = lo.reshape(HEADS, HS, w)

        def scores(h):
            return nn(k2[l, h], q2[h, :, 0:w])

        def soft(h, s):
            p = jnp.exp2(s - jnp.max(s, axis=0, keepdims=True)).astype(BF)
            if l == 0:
                probs0[h, :, tsl] = p
            else:
                probs1[h, :, 0:w] = p
            return p

        def mix(h, p):
            o = nn(vTx[l, h], p)
            inv = 1.0 / o[HS:HS + 1]
            invs[l, h:h + 1, tsl] = inv
            ms[l, h * HS:(h + 1) * HS, tsl] = (o[:HS] * inv).astype(BF)

        n_g = HEADS // GF
        s = [scores(u) for u in range(GF)]
        before = None
        for g in range(n_g):
            s2 = [scores((g + 1) * GF + u) for u in range(GF)] if g + 1 < n_g else None
            ps = [soft(g * GF + u, s[u]) for u in range(GF)]
            if before is not None:
                for u in range(GF):
                    mix((g - 1) * GF + u, before[u])
            s, before = s2, ps
        for u in range(GF):
            mix((n_g - 1) * GF + u, before[u])
        return x + nn(owT[l], ms[l, :, tsl])

    def chunk_out(i, t0, w):
        tsl = pl.ds(t0, w)
        pairs = (
            (nq.at[0, :, tsl], nq_hbm.at[:, tsl]), (qs.at[0, :, tsl], qs_hbm.at[:, tsl]),
            (ms.at[0, :, tsl], ms_hbm.at[:, tsl]), (dus.at[0, :, tsl], dus_hbm.at[:, tsl]),
            (probs0.at[:, :, tsl], probs_hbm.at[:, :, tsl]), (invs.at[0, :, tsl], invs_hbm.at[:, tsl]))
        return [pltpu.make_async_copy(a, b, csem.at[k, i]) for k, (a, b) in enumerate(pairs)]

    def chunk_a(i, t0, w):
        tsl = pl.ds(t0, w)
        ids = idx_ref[:, tsl]
        onehot = (lax.broadcasted_iota(jnp.int32, (TOKS, w), 0) == ids).astype(BF)
        x = wide(gains[3], w) + nn(posT[...], onehot)
        x = fwd_layer(0, x, t0, w)
        x = fwd_layer(1, x, t0, w)
        n, r = norm(x, wide(gains[2], w))
        no[:, tsl] = n
        nT = n.T
        e = nn(nT, hw[...]) - err[tsl, :].astype(F32)
        esum[...] += jnp.sum(e * e, axis=0, keepdims=True)
        eb = e.astype(BF)
        err[tsl, :] = eb
        dn = nt(hw[...], eb)
        dx = norm_back(dn, n, r, wide(gains[2], w))
        du = dx.astype(BF)
        dus[1, :, tsl] = du
        attention_back(du, w, tsl, ow.at[1], invs.at[1], ms.at[1], lambda h: probs1[h, :, 0:w], vx.at[1], kT.at[1],
                       qs.at[1], dme, dqs, dkvT)
        dn = nn(qw[1], dqs[:, tsl])
        dx = dx + norm_back(dn, nq[1, :, tsl], rs[1, :, tsl], wide(gains[1], w))
        dus[0, :, tsl] = dx.astype(BF)
        for cp in chunk_out(i, t0, w):
            cp.start()

    loads[4].wait()
    loads[5].wait()
    full = ROWS // CH
    rem = ROWS - full * CH

    @pl.loop(0, full)
    def _(i):
        chunk_a(i, pl.multiple_of(i * CH, CH), CH)

    chunk_a(full, full * CH, rem)

    loss_ref[...] = jnp.full((8, 128), jnp.sum(esum[...]), F32)
    emit, finish = make_emit(stage, gsem)
    for b in range(2):
        to = pl.ds(64 * b, 64)
        emit(nn, no[b * 256:(b + 1) * 256, :], lambda c: err[:, c:c + 256], 256, PIX, 48, [
            (0, 40, g1_hbm.at[to, pl.ds(24, 40)]), (40, 48, g2_hbm.at[to, pl.ds(32, 8)])])
    emit(nt, nq[1], lambda c: dqs[c:c + 256, :], DD, DD, 16, [(0, 16, g2_hbm.at[:, pl.ds(0, 16)])])
    emit(nt, ms[1], lambda c: dus[1, c:c + 256, :], DD, DD, 16, [(0, 16, g2_hbm.at[:, pl.ds(16, 16)])])
    dT[0:DD, :] = (dkvT[0:DD, :] * SCALE).astype(BF)
    dT[DD:2 * DD, :] = dkvT[DD:2 * DD, :].astype(BF)
    keep.append(pltpu.make_async_copy(dT, d_hbm, ksem.at[3]))
    keep[3].start()
    for b in range(4):
        to = pl.ds(32 * b, 32)
        emit(nt, nfT[1, b * 352:(b + 1) * 352, :], lambda c: dT[c:c + 256, :], 352, 2 * DD, 88, [
            (0, 64, g0_hbm.at[to, pl.ds(0, 64)]), (64, 88, g1_hbm.at[to, pl.ds(0, 24)])])
    finish()
    for cp in keep:
        cp.wait()

    @pl.loop(0, full)
    def _(i):
        for cp in chunk_out(i, pl.multiple_of(i * CH, CH), CH):
            cp.wait()

    for cp in chunk_out(full, full * CH, rem):
        cp.wait()


ROWS_1 = (64, 64, 40)
ROWS_2 = (32, 32, 56)


def compute(features, masked_index, pos_table, mask_token, key_gain, key_weight, query_gain,
            query_weight, out_weight, out_gain, head_weight, target):
    vm = pl.BlockSpec(memory_space=pltpu.VMEM)
    hb = pl.BlockSpec(memory_space=pl.ANY)
    S = jax.ShapeDtypeStruct
    out_shape = (
        S((8, 128), F32), *(S((128, r, 128), F32) for r in ROWS_1),
        S((DD, ROWS), BF), S((DD, ROWS), BF), S((DD, ROWS), BF), S((DD, ROWS), BF),
        S((HEADS, VIS, ROWS), BF), S((HEADS, ROWS), F32),
        S((DD, VIS), BF), S((HEADS, VIS, EXT), BF), S((D, VIS), BF), S((2 * DD, VIS), BF),
    )
    V = pltpu.VMEM
    scratch = [
        V((TOKS, DD), BF), V((2, D, 2 * DD), BF), V((2, DD, DD), BF), V((2, DD, DD), BF), V((DD, PIX), BF),
        V((ROWS, PIX), BF), V((DD, TOKS), BF), V((2, DD, DD), BF), V((2, DD, DD), BF),
        V((2, VIS, D), BF), V((2, D, VIS), BF),
        V((2, HEADS, VIS, 2 * HS), BF), V((2, HEADS, VIS, EXT), BF), V((2, HEADS, EXT, VIS), BF), V((2, DD, VIS), BF),
        V((HEADS, VIS, ROWS), BF), V((HEADS, VIS, CH), BF),
        V((2, DD, ROWS), BF), V((2, DD, ROWS), BF), V((2, DD, ROWS), BF), V((2, DD, ROWS), BF), V((DD, ROWS), BF),
        V((DD, ROWS), BF), V((2, 1, ROWS), F32), V((2, HEADS, ROWS), F32), V((2 * DD, VIS), F32),
        V((4, DD, 128), F32), V((HEADS, 2 * HS, CH), BF), V((HEADS, EXT, CH), BF),
        V((2, SLOT, 128), F32), V((1, PIX), F32), V((2 * DD, VIS), BF),
        pltpu.SemaphoreType.DMA((6,)), pltpu.SemaphoreType.DMA((2, 3)), pltpu.SemaphoreType.DMA((6, NCH)),
        pltpu.SemaphoreType.DMA((4,)),
    ]
    return pl.pallas_call(
        compute_kernel,
        out_shape=out_shape,
        in_specs=[vm] * 6 + [hb] * 6,
        out_specs=[vm] + [hb] * 13,
        scratch_shapes=scratch,
        compiler_params=pltpu.CompilerParams(vmem_limit_bytes=63 * 1024 * 1024),
        name="decode",
    )(
        masked_index, features, mask_token, key_gain, query_gain, out_gain,
        pos_table, key_weight, query_weight, out_weight, head_weight, target,
    )


MESH = pl.DeviceIdType.MESH
PARTS = 3
ORDERS = (("x", "y", "z"), ("y", "z", "x"), ("z", "x", "y"))
HALF_1 = (32, 32, 24)
HALF_2 = (16, 16, 32)


def part_index(coords):
    y = coords["y"]
    if isinstance(y, slice):
        return (y, coords["x"], coords["z"], y)
    return (y // 2, coords["x"], coords["z"], y % 2)


def block_shape(free):
    shape = []
    for name, size in (("y", 2), ("x", 4), ("z", 4), ("y", 2)):
        if name in free:
            shape.append(size)
    return tuple(shape)


def reduce_kernel(
    loss_ref, feat_ref, kgain_ref,
    g0, g1, g2, nq_hbm, qs_hbm, ms_hbm, dus_hbm, probs_hbm, invs_hbm, kT_hbm, vx_hbm, nfT_hbm, d_hbm, ow_hbm, kw_hbm,
    k_out, q_out, o_out, h_out, l_out, fgrad_ref,
    nq, qs, ms, dus, probs0, invs, kT, vx, nfT, d1, ow, kw, dqs, dkvT, dT, dme, stage, lbuf,
    send, recv, lsem, csem, ksem, gsem, *rest,
):
    own1, own2, got1, got2 = (rest[3 * i:3 * i + 3] for i in range(4))
    buffers = rest[12:]
    clip, tok = lax.axis_index("clip"), lax.axis_index("tok")
    me = {"x": clip % 4, "y": (clip // 4) * 2 + (tok // 2) % 2, "z": tok // 4}
    core = tok % 2
    full_slice = slice(None)

    def device(c, k):
        return ((c["y"] // 2) * 4 + c["x"], c["z"] * 4 + (c["y"] % 2) * 2 + k)

    def shifted(axis, by):
        c = dict(me)
        c[axis] = (me[axis] + by + 4) % 4
        return c

    partner = device(me, 1 - core)
    sides = {a: (device(shifted(a, 1), core), device(shifted(a, -1), core)) for a in "xyz"}

    chunks = [(i * CH, min(CH, ROWS - i * CH)) for i in range(NCH)]

    def chunk_in(i, t0, w):
        tsl = pl.ds(t0, w)
        pairs = (
            (dus_hbm.at[:, tsl], dus.at[:, tsl]), (invs_hbm.at[:, tsl], invs.at[:, tsl]),
            (ms_hbm.at[:, tsl], ms.at[:, tsl]), (probs_hbm.at[:, :, tsl], probs0.at[:, :, tsl]),
            (qs_hbm.at[:, tsl], qs.at[:, tsl]), (nq_hbm.at[:, tsl], nq.at[:, tsl]))
        return [pltpu.make_async_copy(a, b, csem.at[k, i]) for k, (a, b) in enumerate(pairs)]

    others = [
        pltpu.make_async_copy(ow_hbm.at[0], ow, ksem.at[0]), pltpu.make_async_copy(vx_hbm, vx, ksem.at[1]),
        pltpu.make_async_copy(kT_hbm, kT, ksem.at[2]), pltpu.make_async_copy(nfT_hbm, nfT, ksem.at[3]),
        pltpu.make_async_copy(d_hbm, d1, ksem.at[4]), pltpu.make_async_copy(kw_hbm, kw, ksem.at[5])]
    for cp in others[0:3]:
        cp.start()
    for cp in chunk_in(0, 0, CH):
        cp.start()

    barrier = pltpu.get_barrier_semaphore()
    for dev in [partner] + [d for a in "xyz" for d in sides[a]]:
        pl.semaphore_signal(barrier, inc=1, device_id=dev, device_id_type=MESH)
    pl.semaphore_wait(barrier, 7)

    counter = [0]

    def remote(src, dst, dev):
        i = counter[0]
        counter[0] += 1
        return pltpu.make_async_remote_copy(
            src_ref=src, dst_ref=dst, send_sem=send.at[i], recv_sem=recv.at[i], device_id=dev, device_id_type=MESH)

    class Group:
        def __init__(self, srcs, owns, gots, own_index, bufs, rows, half, base):
            self.srcs, self.owns, self.gots, self.own_index = srcs, owns, gots, own_index
            self.first, self.second, self.rows, self.half = bufs[0:9], bufs[9:18], rows, half
            self.swaps, self.mine = {}, {}
            k = base
            for by in (2, 1, 3, 0):
                for p in range(PARTS):
                    i = part_index(self.coords(p, 0, self.at(p, 0, by)))
                    self.swaps[p, by] = remote(srcs[p].at[i + (1 - core,)], gots[p].at[i], partner)
                    if base is not None:
                        self.mine[p, by] = pltpu.make_async_copy(srcs[p].at[i + (core,)], owns[p].at[i], lsem.at[k])
                        k += 1
            self.step1, self.step2 = {}, {}
            for s in range(3):
                for p in range(PARTS):
                    a = ORDERS[p][s]
                    far = self.block(p, s, 2)
                    pre = (full_slice,) * len(block_shape(ORDERS[p][s + 1:]))
                    lo, hi = pl.ds(0, half[p]), pl.ds(half[p], rows[p] - half[p])
                    f = self.first[s * 3 + p]
                    self.step1[s, p] = (
                        remote(far.at[pre + (lo,)], f.at[(0,) + pre + (lo,)], sides[a][0]),
                        remote(far.at[pre + (hi,)], f.at[(0,) + pre + (hi,)], sides[a][1]))
                    o = self.second[s * 3 + p]
                    self.step2[s, p] = (
                        remote(self.block(p, s, 1), o.at[0], sides[a][0]),
                        remote(self.block(p, s, 3), o.at[1], sides[a][1]))

        def at(self, p, s, by):
            return (me[ORDERS[p][s]] + by) % 4

        def coords(self, p, s, j):
            c = {}
            for t, a in enumerate(ORDERS[p]):
                c[a] = me[a] if t < s else (j if t == s else full_slice)
            return c

        def block(self, p, s, by):
            return self.owns[p].at[part_index(self.coords(p, s, self.at(p, s, by))) + self.own_index]

        def index(self, p, s, by):
            return part_index(self.coords(p, s, self.at(p, s, by)))

        def free(self, p, s):
            return (full_slice,) * len(block_shape(ORDERS[p][s + 1:]))

        def swap(self):
            for by in (2, 1, 3, 0):
                for p in range(PARTS):
                    self.swaps[p, by].start()
                    if self.mine:
                        self.mine[p, by].start()

        def add_swap(self, by):
            for p in range(PARTS):
                if self.mine:
                    self.mine[p, by].wait()
                self.swaps[p, by].wait_recv()

                i = self.index(p, 0, by)
                self.owns[p][i + self.own_index] = self.owns[p][i + self.own_index] + self.gots[p][i]

        def send_far(self, s):
            for p in range(PARTS):
                for cp in self.step1[s, p]:
                    cp.start()

        def send_near(self, s):
            for p in range(PARTS):
                for cp in self.step1[s, p]:
                    cp.wait_recv()
                lo, hi = pl.ds(0, self.half[p]), pl.ds(self.half[p], self.rows[p] - self.half[p])
                own, f = self.owns[p], self.first[s * 3 + p]
                r, l = self.index(p, s, 1) + self.own_index, self.index(p, s, 3) + self.own_index
                i = (0,) + self.free(p, s)
                own[r + (lo,)] = own[r + (lo,)] + f[i + (lo,)]
                own[l + (hi,)] = own[l + (hi,)] + f[i + (hi,)]
                for cp in self.step2[s, p]:
                    cp.start()

        def collect(self, s):
            for p in range(PARTS):
                for cp in self.step2[s, p]:
                    cp.wait_recv()
                own, o = self.owns[p], self.second[s * 3 + p]
                m = self.index(p, s, 0) + self.own_index
                own[m] = own[m] + o[0] + o[1]

        def finish(self):
            for cp in self.swaps.values():
                cp.wait_send()
            for s in range(3):
                for p in range(PARTS):
                    for cp in self.step1[s, p] + self.step2[s, p]:
                        cp.wait_send()

    one = Group((g0, g1, g2), own1, got1, (), buffers[0:18], ROWS_1, HALF_1, 0)
    two = Group(own2, own2, got2, (core,), buffers[18:36], ROWS_2, HALF_2, None)

    one.swap()
    for i, (t0, w) in enumerate(chunks[1:]):
        for cp in chunk_in(i + 1, t0, w):
            cp.start()
    for cp in others[3:]:
        cp.start()
    lbuf[0, core] = loss_ref[...]
    lcopy = remote(loss_ref, lbuf.at[0, core], partner)
    lcopy.start()

    l_near, l_far = [], []
    for s, axis in enumerate("xyz"):
        mine = lbuf.at[s + 1, me[axis]]
        l_near.append([remote(mine, mine, sides[axis][0]), remote(mine, mine, sides[axis][1])])
        far = lbuf.at[s + 1, (me[axis] + 3) % 4]
        l_far.append(remote(far, far, sides[axis][0]))

    def loss_near(s):
        if s == 0:
            lcopy.wait()
            tile = lbuf[0, 0] + lbuf[0, 1]
        else:
            l_far[s - 1].wait()
            tile = lbuf[s, 0] + lbuf[s, 1] + lbuf[s, 2] + lbuf[s, 3]
        lbuf[s + 1, me["xyz"[s]]] = tile
        for cp in l_near[s]:
            cp.start()

    def loss_far(s):
        for cp in l_near[s]:
            cp.wait()
        l_far[s].start()

    dkvT[...] = jnp.zeros_like(dkvT)
    for cp in others[0:3]:
        cp.wait()

    def chunk_b(i, t0, w):
        tsl = pl.ds(t0, w)
        for cp in chunk_in(i, t0, w):
            cp.wait()
        attention_back(dus[:, tsl], w, tsl, ow, invs, ms, lambda h: probs0[h, :, tsl], vx, kT, qs, dme, dqs, dkvT)

    @pl.loop(0, ROWS // CH)
    def _(i):
        chunk_b(i, pl.multiple_of(i * CH, CH), CH)

        @pl.when(i == 1)
        def _():
            one.add_swap(2)
            one.send_far(0)
            loss_near(0)

        @pl.when(i == 4)
        def _():
            one.add_swap(1)
            one.add_swap(3)

    chunk_b(NCH - 1, *chunks[NCH - 1])
    one.send_near(0)
    loss_far(0)

    emit, flush = make_emit(stage, gsem)
    flat = [o.reshape(128, r, 128) for o, r in zip(own2, ROWS_2)]
    emit(nt, nq[...], lambda c: dqs[c:c + 256, :], DD, DD, 16, [(0, 16, flat[2].at[:, pl.ds(24, 16)])])
    emit(nt, ms[...], lambda c: dus[c:c + 256, :], DD, DD, 16, [(0, 16, flat[2].at[:, pl.ds(40, 16)])])
    dT[0:DD, :] = (dkvT[0:DD, :] * SCALE).astype(BF)
    dT[DD:2 * DD, :] = dkvT[DD:2 * DD, :].astype(BF)
    others[3].wait()
    for b in range(4):
        to = pl.ds(32 * b, 32)
        emit(nt, nfT[b * 352:(b + 1) * 352, :], lambda c: dT[c:c + 256, :], 352, 2 * DD, 88, [
            (0, 32, flat[0].at[to]), (32, 64, flat[1].at[to]), (64, 88, flat[2].at[to, pl.ds(0, 24)])])
    flush()
    two.swap()

    def feature_grad(l, d):
        dn = nt(d.T, kw[l])
        xh, r = feature_norm(feat_ref, l)
        dxh = dn * kgain_ref[l:l + 1, :].astype(F32)
        m1 = jnp.mean(dxh, axis=1, keepdims=True)
        m2 = jnp.mean(dxh * xh, axis=1, keepdims=True)
        fgrad_ref[l] = (r * (dxh - m1 - xh * m2)).astype(BF)

    others[4].wait()
    others[5].wait()
    feature_grad(0, dT[...])
    two.add_swap(2)
    two.send_far(0)
    one.add_swap(0)
    feature_grad(1, d1[...])
    one.collect(0)
    one.send_far(1)
    loss_near(1)
    two.add_swap(1)
    two.add_swap(3)
    two.send_near(0)
    one.send_near(1)
    loss_far(1)
    two.add_swap(0)
    one.collect(1)
    one.send_far(2)
    loss_near(2)
    two.collect(0)
    two.send_far(1)
    one.send_near(2)
    loss_far(2)
    two.send_near(1)
    one.collect(2)
    l_far[2].wait()
    l_out[...] = lbuf[3, 0] + lbuf[3, 1] + lbuf[3, 2] + lbuf[3, 3]
    two.collect(1)
    two.send_far(2)
    two.send_near(2)

    at = part_index(me)

    def rows(group, p, start, n, stride=1):
        own = own1 if group == 1 else own2
        ix = at if group == 1 else at + (core,)
        return own[p][ix + ((pl.ds(start, n, stride=stride)),)] if stride > 1 else own[p][ix + (pl.ds(start, n),)]

    for j in range(8):
        k_out[1, 0:8, j * 128:(j + 1) * 128] = rows(1, 0, j, 8, 8)
        k_out[1, 8:11, j * 128:(j + 1) * 128] = rows(1, 1, j, 3, 8)
    for j in range(4):
        q_out[1, :, j * 128:(j + 1) * 128] = rows(1, 2, j, 4, 4)
        o_out[1, :, j * 128:(j + 1) * 128] = rows(1, 2, 16 + j, 4, 4)
    for r in range(4):
        for j in range(12):
            i = r * 12 + j
            h_out[r:r + 1, j * 128:(j + 1) * 128] = rows(1, 1, 24 + i, 1) if i < 40 else rows(1, 2, i - 8, 1)
    two.collect(2)
    for j in range(8):
        lanes = slice(j * 128, (j + 1) * 128)
        k_out[0, 0:4, lanes] = rows(2, 0, j, 4, 8)
        k_out[0, 4:8, lanes] = rows(2, 1, j, 4, 8)
        k_out[0, 8:11, lanes] = rows(2, 2, j, 3, 8)
    for j in range(4):
        lanes = slice(j * 128, (j + 1) * 128)
        q_out[0, :, lanes] = rows(2, 2, 24 + j, 4, 4)
        o_out[0, :, lanes] = rows(2, 2, 40 + j, 4, 4)
    one.finish()
    two.finish()


def reduce_scatter(state, features, key_gain, key_weight, out_weight):
    V = pltpu.VMEM
    vm = pl.BlockSpec(memory_space=pltpu.VMEM)
    hb = pl.BlockSpec(memory_space=pl.ANY)
    S = jax.ShapeDtypeStruct
    loss, parts, rest = state[0], state[1:4], state[4:]
    grid = (2, 4, 4, 2)
    scratch = [
        V((DD, ROWS), BF), V((DD, ROWS), BF), V((DD, ROWS), BF), V((DD, ROWS), BF),
        V((HEADS, VIS, ROWS), BF), V((HEADS, ROWS), F32),
        V((DD, VIS), BF), V((HEADS, VIS, EXT), BF), V((D, VIS), BF), V((2 * DD, VIS), BF),
        V((DD, DD), BF), V((2, D, 2 * DD), BF), V((DD, ROWS), BF), V((2 * DD, VIS), F32), V((2 * DD, VIS), BF),
        V((HEADS, EXT, CH), BF), V((2, SLOT, 128), F32), V((4, 4, 8, 128), F32),
    ]
    n_copies = 2 * (12 + 36) + 1 + 9
    dma = pltpu.SemaphoreType.DMA
    scratch += [dma((n_copies,)), dma((n_copies,)), dma((12,)), dma((6, NCH)), dma((6,)), dma((2, 3))]
    scratch += [V(grid + (r, 128), F32) for r in ROWS_1] + [V(grid + (2, r, 128), F32) for r in ROWS_2]
    scratch += [V(grid + (r, 128), F32) for r in ROWS_1] + [V(grid + (r, 128), F32) for r in ROWS_2]
    for rows in (ROWS_1, ROWS_2):
        for n in (1, 2):
            for s in range(3):
                for p in range(PARTS):
                    scratch.append(V((n,) + block_shape(ORDERS[p][s + 1:]) + (rows[p], 128), F32))
    return pl.pallas_call(
        reduce_kernel,
        out_shape=(
            S((2, 11, 2 * DD), F32), S((2, 4, DD), F32), S((2, 4, DD), F32), S((4, PIX), F32), S((8, 128), F32),
            S((2, VIS, D), BF),
        ),
        in_specs=[vm] * 3 + [hb] * 15,
        out_specs=[vm] * 6,
        scratch_shapes=scratch,
        compiler_params=pltpu.CompilerParams(
            collective_id=0, has_side_effects=True, vmem_limit_bytes=63 * 1024 * 1024),
        name="reduce",
    )(
        loss, features, key_gain, *(g.reshape(grid + (2,) + g.shape[1:]) for g in parts), *rest, out_weight, key_weight)


def output_kernel(loss, k_in, q_in, o_in, h_in, f_in, loss_out, k_out, q_out, o_out, h_out, f_out):
    loss_out[0, 0] = loss[0, 0] * (1.0 / (128 * ROWS * PIX))
    for a, b in ((f_in, f_out), (k_in, k_out), (q_in, q_out), (o_in, o_out), (h_in, h_out)):
        b[...] = a[...]


def outputs(k, q, o, h, loss, f):
    vm = pl.BlockSpec(memory_space=pltpu.VMEM)
    sm = pl.BlockSpec(memory_space=pltpu.SMEM)
    arrays = (k, q, o, h, f)
    return pl.pallas_call(
        output_kernel,
        out_shape=(jax.ShapeDtypeStruct((1, 1), F32), *(jax.ShapeDtypeStruct(a.shape, a.dtype) for a in arrays)),
        in_specs=[sm] + [vm] * 5,
        out_specs=[sm] + [vm] * 5,
        name="outputs",
    )(loss, *arrays)


def shards(features, masked_index, pos_table, mask_token, key_gain, key_weight, query_gain,
           query_weight, out_weight, out_gain, head_weight, target):
    state = compute(
        features, masked_index, pos_table, mask_token, key_gain, key_weight, query_gain,
        query_weight, out_weight, out_gain, head_weight, target)
    summed = reduce_scatter(state, features, key_gain, key_weight, out_weight)
    loss, key_grad, query_grad, out_grad, head_grad, feature_grad = outputs(*summed)
    return loss[0, 0], feature_grad, key_grad, query_grad, out_grad, head_grad


def solution(mesh):
    both = ("clip", "tok")
    in_specs = (
        P(None, both, None), P(both, None), P(), P(), P(), P(), P(), P(), P(), P(), P(), P(both, None, None))
    out_specs = (
        P(), P(None, both, None), P(None, both, None), P(None, both, None), P(None, both, None), P(both, None))
    return jax.shard_map(shards, mesh=mesh, in_specs=in_specs, out_specs=out_specs, check_vma=False)
```

time: 158 us -> 141 us (0.89)
  local copies, waits for them, and re-layouts: 9.32 us -> 1.61 us
  Pallas kernels: 146 us -> 139 us
  between operations: 2.43 us -> 0.66 us
    pallas_call x1, Pallas kernels: 81.7 us -> 65 us  [compute(): pl.pallas_call(compute_kernel, out_shape=out_shape, in_specs=[vm] * 6 + [...]
    pallas_call x1 -> x2, Pallas kernels: 63.8 us -> 73.8 us  [the longest x1 71.4 us: reduce_scatter(): pl.pallas_call(reduce_kernel, out_shape=(S((2, 11, 2 * DD), F32), S((2, 4...]
    unnamed x4 -> x1, local copies, waits for them, and re-layouts: 5.6 us -> 1.61 us
    reshape x2 -> x0, local copies, waits for them, and re-layouts: 2.52 us -> none  [the longest x1 1.26 us: compute(): mask_token.reshape(1, DD)]
where the time goes in v2:
time: 141 us
  Pallas kernels  139 us (99%)
  local copies, waits for them, and re-layouts  1.61 us (1%)
    pallas_call x1, Pallas kernels, reduce_scatter(): pl.pallas_call(reduce_kernel, out_shape=(S((2, 11, 2 * DD), F32), S((2, 4...  71.4 us
    pallas_call x1, Pallas kernels, compute(): pl.pallas_call(compute_kernel, out_shape=out_shape, in_specs=[vm] * 6 + [...  65 us

profile of v2, /device:TPU:0, one launch (start us, length us, event | category | flops | bytes accessed | tf_op | source)
XLA Modules:
  0.0 141.1 jit_solution(2973281593265740325)
XLA Ops:
  0.6 65.0 %decode.1 = (f32[8,128]{1,0:T(8,128)}, f32[128,64,128]{2,1,0:T(8,128)}, f32[128,64,128]{2,1,0:T(8,128)}, f32[128,40,128]{2,1,0:T(8,128)}, bf16[512,1408]{1,0:T(8...) custom-call(s32[1,1408]{1,0:T(1,128)} %idx_ref.1, ...), custom_call_target="tpu_custom_call" | custom-call | tf_op jit(solution)/shard_map/decode/pallas_call | solution.py:333
  65.7 71.4 %reduce.1 = (f32[2,11,1024]{2,1,0:T(8,128)}, f32[2,4,512]{2,1,0:T(4,128)}, f32[2,4,512]{2,1,0:T(4,128)}, f32[4,1536]{1,0:T(4,128)}, f32[8,128]{1,0:T(8,128)}, /*index=5*/bf16[2,160,1408]{2,1,0:T(8,128)(2,1)}) custom-call(f32[8,128]{1,0:T(8,128)} %get-tuple-element.32.loss_ref, bf16[2,160,1408]{2,1,0:T(8,128)(2,1)} %feat_ref.3, bf16[2,1408]{1,0:T(2,128)(2,1)} %kgain_ref.3, ...), custom_call_target="tpu_custom_call" | custom-call | tf_op jit(solution)/shard_map/reduce/pallas_call | solution.py:696
  137.1 2.3 %outputs.1 = (f32[1,1]{1,0:T(1,128)}, f32[2,11,1024]{2,1,0:T(8,128)}, f32[2,4,512]{2,1,0:T(4,128)}, f32[2,4,512]{2,1,0:T(4,128)}, f32[4,1536]{1,0:T(4,128)}, /*index=5*/bf16[2,160,1408]{2,1,0:T(8,128)(2,1)}) custom-call(f32[8,128]{1,0:T(8,128)} %get-tuple-element.46.loss, f32[2,11,1024]{2,1,0:T(8,128)} %get-tuple-element.47.k_in, ...), custom_call_target="tpu_custom_call" | custom-call | tf_op jit(solution)/shard_map/outputs/pallas_call | solution.py:722
  139.5 1.6 %copy.18 = f32[2,11,1024]{2,0,1:T(2,128)} copy(f32[2,11,1024]{2,1,0:T(8,128)} %get-tuple-element.60) | data formatting | bytes 180224
